TPU v7x, 128 devices: a whole 4x4x4 slice. The times are simulated.
128 devices in a mesh: dp: 16 (over x, y_hi, core), shard: 8 (over y_lo, z).
Axes of the slice: x: 4, y: 4 (y_hi: 2, y_lo: 2; y = y_hi * 2 + y_lo), z: 4, core: 2. Of those that a mesh axis runs over, the one named last changes fastest.
Arguments:
- gradients: bfloat16 [16, 3968, 3968], P('dp', None, 'shard'), may hold values from -12 to 12
- error_memory: float32 [16, 3968, 3968], P('dp', None, 'shard'), may hold values from -9 to 9
- q_factor: bfloat16 [3968, 1024], P('shard'), may hold values from -0.09375 to 0.09375
Outputs:
- rebuilt: bfloat16 [3968, 3968], P(None, 'shard')
- new_error: float32 [16, 3968, 3968], P('dp', None, 'shard')
All inputs are finite; a program needn't handle non-finite values.
Results may differ from a plain program's by a relative error of at most 0.0072.
Values may be sent and summed in bfloat16 or wider, within the bound.
No kernel may reach another device: no remote copies, remote signals or barrier semaphores. Data moves between devices by JAX's collectives and lax.ppermute only.
A program may use at most 192 MiB of HBM per device.

v0:
```python
import functools

import jax
import jax.numpy as jnp
from jax import lax
from jax.experimental import pallas as pl
from jax.experimental.pallas import tpu as pltpu
from jax.sharding import Mesh, PartitionSpec as P

f32 = jnp.float32
bf16 = jnp.bfloat16
HIGHEST = lax.Precision.HIGHEST
HIGH = lax.Precision.HIGH

CHIPS = ("x", "yh")
CORE = "c"
SHARD = ("yl", "z")
DP = CHIPS + (CORE,)
SWAP = [(0, 1), (1, 0)]

TILE, LANES = 8, 128
MIB = 2**20


def dot(a, b, dims, precision=HIGHEST):
    return lax.dot_general(a, b, (dims, ((), ())), precision=precision, preferred_element_type=f32)


def spread(a, axes, n):
    blocks = jnp.broadcast_to(a[None], (n,) + a.shape)
    return lax.all_to_all(blocks, axes, 0, 0, tiled=True)


def cut_kernel(rows, core_ref, g_ref, e_ref, mine_ref, other_ref):
    core = core_ref[0]
    width = mine_ref.shape[2]
    combined = g_ref[...].astype(f32) + e_ref[...]
    at = pl.program_id(0) * 2 * width + lax.broadcasted_iota(jnp.int32, combined.shape, 1)
    combined = jnp.where(at < rows, combined, 0.0).astype(bf16)
    low, high = combined[:, :width], combined[:, width:]

    @pl.when(core == 0)
    def _():
        mine_ref[0], other_ref[0] = low, high

    @pl.when(core != 0)
    def _():
        mine_ref[0], other_ref[0] = high, low


def cut(core, gradient_t, error_t, n_chips, width):
    cols, rows = gradient_t.shape
    whole = pl.BlockSpec((cols, 2 * width), lambda i, core: (0, i))
    part = pl.BlockSpec((1, cols, width), lambda i, core: (i, 0, 0))
    shape = jax.ShapeDtypeStruct((n_chips, cols, width), bf16)
    return pl.pallas_call(
        functools.partial(cut_kernel, rows),
        grid_spec=pltpu.PrefetchScalarGridSpec(
            num_scalar_prefetch=1, grid=(n_chips,), in_specs=[whole, whole], out_specs=[part, part]
        ),
        out_shape=[shape, shape],
        compiler_params=pltpu.CompilerParams(vmem_limit_bytes=48 * MIB),
        name="cut",
    )(core[None], gradient_t, error_t)


def finish_kernel(core_ref, near_ref, far_ref, x_near_ref, x_far_ref, g_ref, e_ref, rebuilt_ref, error_ref, x):
    core = core_ref[0]
    n_sh, _, depth, width = near_ref.shape
    cols = g_ref.shape[0]
    n_chips, band, _ = x_near_ref.shape

    @pl.when(pl.program_id(0) == 0)
    def _():
        for i in range(n_chips):
            x[pl.ds(pl.multiple_of((2 * i + core) * band, band), band)] = x_near_ref[i]
            x[pl.ds(pl.multiple_of((2 * i + 1 - core) * band, band), band)] = x_far_ref[i]

    def store(columns, ref):
        value = dot(x[:cols], ref[:, 0].reshape(n_sh * depth, width), ((1,), (0,)), None)
        rebuilt_ref[:, columns] = value.astype(bf16)
        error_ref[:, columns] = g_ref[:, columns].astype(f32) + e_ref[:, columns] - value

    low, high = pl.ds(0, width), pl.ds(width, width)

    @pl.when(core == 0)
    def _():
        store(low, near_ref)
        store(high, far_ref)

    @pl.when(core != 0)
    def _():
        store(low, far_ref)
        store(high, near_ref)


def finish(core, near, far, x_near, x_far, gradient_t, error_t):
    cols, rows = gradient_t.shape
    n_sh, n_chips, depth, width = near.shape
    whole = pl.BlockSpec((cols, 2 * width), lambda i, core: (0, i))
    part = pl.BlockSpec((n_sh, 1, depth, width), lambda i, core: (0, i, 0, 0))
    fixed = pl.BlockSpec(x_near.shape, lambda i, core: (0, 0, 0))
    return pl.pallas_call(
        finish_kernel,
        grid_spec=pltpu.PrefetchScalarGridSpec(
            num_scalar_prefetch=1,
            grid=(n_chips,),
            in_specs=[part, part, fixed, fixed, whole, whole],
            out_specs=[whole, whole],
            scratch_shapes=[pltpu.VMEM((n_chips * 2 * x_near.shape[1], x_near.shape[2]), bf16)],
        ),
        out_shape=[
            jax.ShapeDtypeStruct((cols, rows), bf16),
            jax.ShapeDtypeStruct((cols, rows), f32),
        ],
        compiler_params=pltpu.CompilerParams(vmem_limit_bytes=20 * MIB),
        name="finish",
    )(core[None], near, far, x_near, x_far, gradient_t, error_t)


def add_gram(p, g_ref):
    wide = 2 * LANES
    for i in range(0, p.shape[0], wide):
        g_ref[i : i + wide, i:] += dot(p[i : i + wide], p[i:], ((1,), (1,)), None)


def inverse_factor(block, held):
    n = LANES // TILE
    sub = lax.broadcasted_iota(jnp.int32, (TILE, LANES), 0)
    lane = lax.broadcasted_iota(jnp.int32, (TILE, LANES), 1)
    full = lambda v: jnp.broadcast_to(v, (TILE, LANES))
    scale = full(full(block[:TILE, :1])[:1])
    root = lax.rsqrt(scale)
    scale = 1.0 / scale
    panel = [block[TILE * t : TILE * (t + 1)] * scale for t in range(n)]
    out = []
    for t in range(n):
        at = TILE * t
        pivot_lanes = (lane >= at) & (lane < at + TILE)
        column = lambda p: [full(panel[p][:, at + k : at + k + 1]) for k in range(TILE)]
        cols = column(t)
        for k in range(TILE):
            held[k] = cols[k]
        s = [[full(held[k, i : i + 1]) for k in range(i + 1)] for i in range(TILE)]
        later = range(t + 1, n)
        e = {p: column(p) for p in later}
        for p in later:
            panel[p] = jnp.where(pivot_lanes, 0.0, panel[p])
        own = jnp.where(pivot_lanes, jnp.where(lane == sub + at, 1.0, 0.0), panel[t])
        held[TILE] = own
        rows = [full(held[TILE, k : k + 1]) for k in range(TILE)]
        pivots = result = None
        steps = []
        for k in range(0, TILE, 2):
            d0, d1, d2 = s[k][k], s[k + 1][k], s[k + 1][k + 1]
            det = d0 * d2 - d1 * d1
            inv = 1.0 / det
            q = {i: (s[i][k] * d2 - s[i][k + 1] * d1, s[i][k + 1] * d0 - s[i][k] * d1) for i in range(k + 2, TILE)}
            m = {i: (q[i][0] * inv, q[i][1] * inv) for i in q}
            for i in q:
                for c in range(k + 2, i + 1):
                    s[i][c] = s[i][c] - (q[i][0] * s[c][k] + q[i][1] * s[c][k + 1]) * inv
            r0, r1 = rows[k], rows[k + 1]
            v0, v1 = (d2 * r0 - d1 * r1) * inv, (d0 * r1 - d1 * r0) * inv
            steps.append((v0, v1, m))
            for i in q:
                rows[i] = rows[i] - (m[i][0] * r0 + m[i][1] * r1)
            for p in later[:1]:
                e0, e1 = e[p][k], e[p][k + 1]
                panel[p] = panel[p] - (e0 * v0 + e1 * v1)
                for i in q:
                    e[p][i] = e[p][i] - (m[i][0] * e0 + m[i][1] * e1)
            first = 1.0 / d0
            pivots = d0 if k == 0 else jnp.where(sub == k, d0, pivots)
            pivots = jnp.where(sub == k + 1, det * first, pivots)
            result = r0 if k == 0 else jnp.where(sub == k, r0, result)
            result = jnp.where(sub == k + 1, r1 - (d1 * first) * r0, result)
        out.append(jnp.where(lane < at + TILE, result * (lax.rsqrt(pivots) * root), 0.0))
        if t + 2 < n:
            v = [None] * TILE
            for k in reversed(range(0, TILE, 2)):
                v[k], v[k + 1], m = steps[k // 2]
                for i in m:
                    v[k] = v[k] - m[i][0] * v[i]
                    v[k + 1] = v[k + 1] - m[i][1] * v[i]
            for p in later[1:]:
                terms = [e[p][k] * v[k] for k in range(TILE)]
                while len(terms) > 1:
                    terms = [x + y for x, y in zip(terms[::2], terms[1::2])]
                panel[p] = panel[p] - terms[0]
    return out


def factor_kernel(near_hbm, far_hbm, u_ref, inverse_ref, a, near, far, held, sems):
    n_sh, n_chips, depth, width = near_hbm.shape
    rank = n_sh * depth
    near_copy = pltpu.make_async_copy(near_hbm, near, sems.at[0])
    far_copy = pltpu.make_async_copy(far_hbm, far, sems.at[1])
    near_copy.start()
    far_copy.start()
    a[...] = jnp.zeros_like(a)
    near_copy.wait()

    @pl.loop(0, n_chips)
    def _(i):
        add_gram(near[:, i].reshape(rank, width), a)

    far_copy.wait()

    @pl.loop(0, n_chips)
    def _(i):
        add_gram(far[:, i].reshape(rank, width), a)

    step, pair = LANES, 2 * LANES
    rc = ((1,), (0,))

    @pl.loop(0, rank // step)
    def _(j):
        r0 = pl.multiple_of(j * step, step)
        side = pl.multiple_of(lax.rem(j, 2) * step, step)
        for t, panel in enumerate(inverse_factor(a[pl.ds(r0, step), pl.ds(r0, step)], held)):
            inverse_ref[pl.ds(pl.multiple_of(r0 + TILE * t, TILE), TILE), pl.ds(side, step)] = panel
        inverse = inverse_ref[pl.ds(r0, step), pl.ds(side, step)]

        @pl.loop((j + 1) // 2, rank // pair)
        def _(c):
            at = pl.multiple_of(c * pair, pair)
            u_ref[pl.ds(r0, step), pl.ds(at, pair)] = dot(inverse, a[pl.ds(r0, step), pl.ds(at, pair)], rc)

        @pl.when(lax.rem(j, 2) == 0)
        def _():
            r1 = pl.multiple_of((j + 1) * step, step)
            ut = u_ref[pl.ds(r0, step), pl.ds(r1, step)].T
            inverse_ref[pl.ds(r0, step), step:] = jnp.zeros((step, step), f32)

            @pl.loop(j // 2, rank // pair)
            def _(c):
                at = pl.multiple_of(c * pair, pair)
                a[pl.ds(r1, step), pl.ds(at, pair)] -= dot(ut, u_ref[pl.ds(r0, step), pl.ds(at, pair)], rc)

        @pl.when(lax.rem(j, 2) == 1)
        def _():
            p0 = pl.multiple_of((j - 1) * step, pair)
            before = inverse_ref[pl.ds(p0, step), :step]
            cross = dot(u_ref[pl.ds(p0, step), pl.ds(r0, step)], before, ((0,), (0,)))
            inverse_ref[pl.ds(r0, step), :step] = -dot(inverse, cross, rc)

            @pl.loop((j + 1) // 2, rank // pair)
            def _(i):
                r1 = pl.multiple_of(i * pair, pair)
                ut = u_ref[pl.ds(p0, pair), pl.ds(r1, pair)].T

                @pl.loop(i, rank // pair)
                def _(c):
                    at = pl.multiple_of(c * pair, pair)
                    a[pl.ds(r1, pair), pl.ds(at, pair)] -= dot(ut, u_ref[pl.ds(p0, pair), pl.ds(at, pair)], rc)

def factor(near, far):
    rank = near.shape[0] * near.shape[2]
    return pl.pallas_call(
        factor_kernel,
        out_shape=[
            jax.ShapeDtypeStruct((rank, rank), f32),
            jax.ShapeDtypeStruct((rank, 2 * LANES), f32),
        ],
        in_specs=[pl.BlockSpec(memory_space=pl.ANY)] * 2,
        out_specs=[pl.BlockSpec(memory_space=pltpu.VMEM)] * 2,
        scratch_shapes=[
            pltpu.VMEM((rank, rank), f32),
            pltpu.VMEM(near.shape, bf16),
            pltpu.VMEM(far.shape, bf16),
            pltpu.VMEM((TILE + 1, TILE, LANES), f32),
            pltpu.SemaphoreType.DMA((2,)),
        ],
        compiler_params=pltpu.CompilerParams(vmem_limit_bytes=28 * MIB),
        cost_estimate=pl.CostEstimate(flops=60_000_000_000, bytes_accessed=8 * rank * rank, transcendentals=0),
        name="factor",
    )(near, far)


def solve_kernel(scale, w_ref, u_ref, inverse_ref, x_ref, y, w):
    pair = 2 * LANES
    rank = u_ref.shape[0]
    n = rank // pair
    block = lambda j: slice(j * pair, (j + 1) * pair)
    for j in range(n):
        value = w_ref[:, block(j)]
        if j:
            value = value - dot(y[:, : j * pair], u_ref[: j * pair, block(j)], ((1,), (0,)), HIGH)
        y[:, block(j)] = dot(value, inverse_ref[block(j), :], ((1,), (1,)), HIGH)
    for j in reversed(range(n)):
        value = y[:, block(j)]
        if j < n - 1:
            value = value - dot(w[:, (j + 1) * pair :], u_ref[block(j), (j + 1) * pair :], ((1,), (1,)), HIGH)
        x = dot(value, inverse_ref[block(j), :], ((1,), (0,)), HIGH)
        w[:, block(j)] = x
        x_ref[:, block(j)] = (x * scale).astype(bf16)


def solve(w, u, inverse, scale):
    return pl.pallas_call(
        functools.partial(solve_kernel, scale),
        out_shape=jax.ShapeDtypeStruct(w.shape, bf16),
        in_specs=[pl.BlockSpec(memory_space=pltpu.VMEM)] * 3,
        out_specs=pl.BlockSpec(memory_space=pltpu.VMEM),
        scratch_shapes=[pltpu.VMEM(w.shape, f32)] * 2,
        compiler_params=pltpu.CompilerParams(vmem_limit_bytes=16 * MIB),
        cost_estimate=pl.CostEstimate(flops=8_000_000_000, bytes_accessed=16 * 2**20, transcendentals=0),
        name="solve",
    )(w, u, inverse)


def shards(gradients, error_memory, q_factor):
    core = lax.axis_index(CORE)
    n_chips = lax.axis_size(CHIPS)
    n_dp = 2 * n_chips
    n_sh = lax.axis_size(SHARD)
    rows, cols = gradients.shape[1:]
    rank = q_factor.shape[1]
    own = -(-rows // (n_dp * LANES)) * LANES
    wide = -(-cols // (n_dp * 16)) * n_dp * 16
    gradient_t, error_t = gradients[0].T, error_memory[0].T

    with jax.named_scope("total"):
        mine, other = cut(core, gradient_t, error_t, n_chips, own)
        got = lax.ppermute(other, CORE, SWAP)
        pair = (mine.astype(f32) + got.astype(f32)).astype(bf16)
        arrived = lax.all_to_all(pair, CHIPS, 0, 0, tiled=True)
        total_t = jnp.sum(arrived.astype(f32), axis=0)

    with jax.named_scope("left"):
        part = dot(q_factor.astype(f32), total_t, ((0,), (0,))).astype(bf16)
        arrived = lax.all_to_all(part.reshape(n_sh, rank // n_sh, own), SHARD, 0, 0, tiled=True)
        p_own = jnp.sum(arrived.astype(f32), axis=0).astype(bf16)
        p_near = spread(p_own, SHARD + CHIPS, n_sh * n_chips).reshape(n_sh, n_chips, rank // n_sh, own)
        p_far = lax.ppermute(p_near, CORE, SWAP)

    with jax.named_scope("right"):
        p_t = lax.dynamic_index_in_dim(p_near, lax.axis_index(CHIPS), 1, keepdims=False).reshape(rank, own)
        total_wide = jnp.pad(total_t, ((0, wide - cols), (0, 0)))
        w_part = dot(total_wide, p_t.astype(f32), ((1,), (1,)), HIGH)
        w_parts = lax.all_to_all(w_part.reshape(n_dp, wide // n_dp, rank), DP, 0, 0, tiled=True)

    with jax.named_scope("solve"):
        u, inverse = factor(p_near, p_far)
        w_parts, inverse = lax.optimization_barrier((w_parts, inverse))
        x_own = solve(jnp.sum(w_parts, axis=0), u, inverse, 1.0 / n_dp)

    with jax.named_scope("rebuild"):
        x_near = spread(x_own, CHIPS, n_chips)
        x_far = lax.ppermute(x_near, CORE, SWAP)
        rebuilt_t, new_error_t = finish(core, p_near, p_far, x_near, x_far, gradient_t, error_t)
    return (rebuilt_t.T, new_error_t.T[None])


def solution(mesh):
    fine = Mesh(mesh.devices.reshape(4, 2, 2, 2, 4), ("x", "yh", "c", "yl", "z"))
    in_specs = (P(DP, None, SHARD), P(DP, None, SHARD), P(SHARD, None))
    out_specs = (P(None, SHARD), P(DP, None, SHARD))
    return jax.shard_map(shards, mesh=fine, in_specs=in_specs, out_specs=out_specs, check_vma=False)
```

profile of v0, /device:TPU:1, one launch (start us, length us, event | category | flops | bytes accessed | tf_op | source)
XLA Modules:
  0.0 217.0 jit_solution(4028693320742354737)
XLA Ops:
  0.6 0.0 copy-start
  0.7 7.3 %cut.1 = (bf16[8,496,256]{2,1,0:T(8,128)(2,1)S(1)}, bf16[8,496,256]{2,1,0:T(8,128)(2,1)S(1)}) custom-call(s32[1]{0:T(128)} %bitcast.core_ref, bf16[496,3968]{1,0:T(8,128)(2,1)} %bitcast.30, f32[496,3968]{1,0:T(8,128)} %bitcast.26), custom_call_target="tpu_custom_call" | custom-call | tf_op jit(solution)/shard_map/total/cut/pallas_call | solution.py:56
  7.9 1.5 collective-permute-start
  9.4 3.7 %collective-permute-done = bf16[8,496,256]{2,1,0:T(8,128)(2,1)S(1)} collective-permute-done((bf16[8,496,256]{2,1,0:T(8,128)(2,1)S(1)}, bf16[8,496,256]{2,1,0:T(8,128)(2,1)S(1)}, u32[]{:S(2)}, u32[]{:S(2)}) %collective-permute-start) | collective-permute-done | bytes 2031648 | tf_op jit(solution)/shard_map/total/ppermute | solution.py:326
  13.1 0.6 add_convert_fusion
  13.7 32.9 %all_to_all.25 = bf16[8,496,256]{2,1,0:T(8,128)(2,1)S(1)} all-to-all(bf16[8,496,256]{2,1,0:T(8,128)(2,1)S(1)} %add_convert_fusion), channel_id=1, replica_groups=mesh['x'=4,'yh'=2,'c'=2,'yl'=2,'z'=4] {'x','yh'}, dimensions={0} | all-to-all | bytes 4063232 | tf_op jit(solution)/shard_map/total/all_to_all | solution.py:328
  46.7 0.3 convert_reduce_fusion
  46.9 0.0 copy-done
  46.9 1.0 fusion
  48.0 0.1 copy.11
  48.1 12.5 %all_to_all.26 = bf16[8,128,256]{1,2,0:T(8,128)(2,1)S(1)} all-to-all(bf16[8,128,256]{1,2,0:T(8,128)(2,1)S(1)} %bitcast.33), channel_id=1, replica_groups=mesh['x'=4,'yh'=2,'c'=2,'yl'=2,'z'=4] {'yl','z'}, dimensions={0} | all-to-all | bytes 1048576 | tf_op jit(solution)/shard_map/left/all_to_all | solution.py:333
  60.5 0.1 reduce_sum.31
  60.6 0.1 copy.7
  60.7 0.5 broadcast_in_dim.9
  61.2 54.4 %all_to_all.27 = bf16[64,128,256]{2,1,0:T(8,128)(2,1)} all-to-all(bf16[64,128,256]{2,1,0:T(8,128)(2,1)S(1)} %broadcast_in_dim.9), channel_id=1, replica_groups=mesh['x'=4,'yh'=2,'c'=2,'yl'=2,'z'=4] {'yl','z','x','yh'}, dimensions={0} | all-to-all | bytes 8388608 | tf_op jit(solution)/shard_map/left/all_to_all | solution.py:31
  115.6 4.5 %collective-permute-start.1 = (bf16[8,8,128,256]{3,2,1,0:T(8,128)(2,1)}, bf16[8,8,128,256]{3,2,1,0:T(8,128)(2,1)}, u32[]{:S(2)}, u32[]{:S(2)}) collective-permute-start(bf16[8,8,128,256]{3,2,1,0:T(8,128)(2,1)} %bitcast.6.near_hbm.near_ref), channel_id=1, source_target_pairs={{0,8},{8,0},{1,9},{9,1},{2,10},{10,2},{3,11},{11,3},{4,12},{12,4},... | collective-permute-start | bytes 12582920 | tf_op jit(solution)/shard_map/left/ppermute | solution.py:336
  120.1 1.1 constant_dynamic-slice_fusion
  121.2 2.1 fusion.1
  123.3 4.5 %all-to-all-start.3 = ((f32[16,32,1024]{2,1,0:T(8,128)}), f32[16,32,1024]{2,1,0:T(8,128)}, u32[]{:S(2)}, u32[]{:S(2)}) async-start(f32[16,32,1024]{2,1,0:T(8,128)} %fusion.1), calls=%async_computation.3 | async-start | bytes 4194304 | tf_op jit(solution)/shard_map/right/all_to_all | solution.py:342
  127.8 0.0 collective-permute-done.1.far_hbm.far_ref
  127.8 48.0 %factor.1 = (f32[1024,1024]{1,0:T(8,128)S(1)}, f32[1024,256]{1,0:T(8,128)S(1)}) custom-call(bf16[8,8,128,256]{3,2,1,0:T(8,128)(2,1)} %bitcast.6.near_hbm.near_ref, bf16[8,8,128,256]{3,2,1,0:T(8,128)(2,1)} %collective-permute-done.1.far_hbm.far_ref), custom_call_target="tpu_custom_call" | custom-call | flops 60000002048 | bytes 8388608 | tf_op jit(solution)/shard_map/solve/factor/pallas_call | solution.py:260
  175.9 0.0 copy-start.2
  175.9 2.0 copy-done.2
  177.9 0.0 all-to-all-done.3
  177.9 1.7 reduce_sum.32.w_ref
  179.6 0.0 slice-start
  179.6 0.0 copy-start.3
  179.6 2.3 %copy-done.3 = f32[1024,1024]{1,0:T(8,128)S(1)} copy-done((f32[1024,1024]{1,0:T(8,128)S(1)}, f32[1024,1024]{1,0:T(8,128)}, u32[]{:S(2)}) %copy-start.3) | copy-done | bytes 4194328
  182.0 0.0 slice-start.1
  182.0 0.0 copy-start.1
  182.0 3.6 %solve.1 = bf16[32,1024]{1,0:T(8,128)(2,1)S(1)} custom-call(f32[32,1024]{1,0:T(8,128)S(1)} %reduce_sum.32.w_ref, f32[1024,1024]{1,0:T(8,128)S(1)} %copy-done.3, f32[1024,256]{1,0:T(8,128)S(1)} %get-tuple-element.15.inverse_ref), custom_call_target="tpu_custom_call" | custom-call | flops 8000000000 | bytes 16777216 | tf_op jit(solution)/shard_map/solve/solve/pallas_call | solution.py:301
  185.6 0.1 broadcast_in_dim.10
  185.7 16.0 %all_to_all.28.x_near_ref = bf16[8,32,1024]{2,1,0:T(8,128)(2,1)S(1)} all-to-all(bf16[8,32,1024]{2,1,0:T(8,128)(2,1)S(1)} %broadcast_in_dim.10), channel_id=1, replica_groups=mesh['x'=4,'yh'=2,'c'=2,'yl'=2,'z'=4] {'x','yh'}, dimensions={0} | all-to-all | bytes 1048576 | tf_op jit(solution)/shard_map/rebuild/all_to_all | solution.py:31
  201.6 2.3 %collective-permute-start.2 = (bf16[8,32,1024]{2,1,0:T(8,128)(2,1)S(1)}, bf16[8,32,1024]{2,1,0:T(8,128)(2,1)S(1)}, u32[]{:S(2)}, u32[]{:S(2)}) collective-permute-start(bf16[8,32,1024]{2,1,0:T(8,128)(2,1)S(1)} %all_to_all.28.x_near_ref), channel_id=1, source_target_pairs={{0,8},{8,0},{1,9},{9,1},{2,10},{10,2},{3,11},{11,3},{4,12},{12,4},... | collective-permute-start | bytes 1572872 | tf_op jit(solution)/shard_map/rebuild/ppermute | solution.py:351
  203.9 1.5 collective-permute-done.2.x_far_ref
  205.4 0.0 slice-done
  205.4 0.0 slice-done.1
  205.4 0.0 copy-done.1
  205.4 11.5 %finish.1 = (bf16[496,3968]{1,0:T(8,128)(2,1)}, f32[496,3968]{1,0:T(8,128)}) custom-call(s32[1]{0:T(128)} %bitcast.core_ref, bf16[8,8,128,256]{3,2,1,0:T(8,128)(2,1)} %bitcast.6.near_hbm.near_ref, bf16[8,8,128,256]{3,2,1,0:T(8,128)(2,1)} %collective-permute-done.1.far_hbm.far_ref, bf16[8,32,1024]{2,1,0:T(8,128)(2,1)S(1)} %all_to_all.28.x_near_ref, ...), custom_call_target="tpu_custom_call" | custom-call | tf_op jit(solution)/shard_map/rebuild/finish/pallas_call | solution.py:103
  (2 shorter events, 0.0 us)
Async XLA Ops:
  0.6 46.3 %copy-start = (bf16[496,1024]{1,0:T(8,128)(2,1)S(1)}, bf16[496,1024]{1,0:T(8,128)(2,1)}, u32[]{:S(2)}) copy-start(bf16[496,1024]{1,0:T(8,128)(2,1)} %param.5) | copy-start | bytes 3047428
  7.9 5.2 %collective-permute-start = (bf16[8,496,256]{2,1,0:T(8,128)(2,1)S(1)}, bf16[8,496,256]{2,1,0:T(8,128)(2,1)S(1)}, u32[]{:S(2)}, u32[]{:S(2)}) collective-permute-start(bf16[8,496,256]{2,1,0:T(8,128)(2,1)S(1)} %get-tuple-element.11), channel_id=1, source_target_pairs={{0,8},{8,0},{1,9},{9,1},{2,10},{10,2},{3,11},{11,3},{4,12},{12,4},... | collective-permute-start | bytes 6094856 | tf_op jit(solution)/shard_map/total/ppermute | solution.py:326
  115.6 12.2 %collective-permute-start.1 = (bf16[8,8,128,256]{3,2,1,0:T(8,128)(2,1)}, bf16[8,8,128,256]{3,2,1,0:T(8,128)(2,1)}, u32[]{:S(2)}, u32[]{:S(2)}) collective-permute-start(bf16[8,8,128,256]{3,2,1,0:T(8,128)(2,1)} %bitcast.6.near_hbm.near_ref), channel_id=1, source_target_pairs={{0,8},{8,0},{1,9},{9,1},{2,10},{10,2},{3,11},{11,3},{4,12},{12,4},... | collective-permute-start | bytes 12582920 | tf_op jit(solution)/shard_map/left/ppermute | solution.py:336
  123.3 54.6 %all-to-all-start.3 = ((f32[16,32,1024]{2,1,0:T(8,128)}), f32[16,32,1024]{2,1,0:T(8,128)}, u32[]{:S(2)}, u32[]{:S(2)}) async-start(f32[16,32,1024]{2,1,0:T(8,128)} %fusion.1), calls=%async_computation.3 | async-start | bytes 4194304 | tf_op jit(solution)/shard_map/right/all_to_all | solution.py:342
  175.9 2.0 copy-start.2
  179.6 25.8 %slice-start = ((s8[7872512]{0:T(1024)(128)(4,1)}), s8[4194304]{0:T(1024)(128)(4,1)S(1)}, s32[]{:S(2)}) async-start(s8[7872512]{0:T(1024)(128)(4,1)} %bitcast.27), calls=%async_computation.5 | async-start | bytes 8388608
  179.6 2.3 %copy-start.3 = (f32[1024,1024]{1,0:T(8,128)S(1)}, f32[1024,1024]{1,0:T(8,128)}, u32[]{:S(2)}) copy-start(f32[1024,1024]{1,0:T(8,128)} %copy-done.2) | copy-start | bytes 12582916
  182.0 23.5 %slice-start.1 = ((s8[7872512]{0:T(1024)(128)(4,1)}), s8[3678208]{0:T(1024)(128)(4,1)S(1)}, s32[]{:S(2)}) async-start(s8[7872512]{0:T(1024)(128)(4,1)} %bitcast.27), calls=%async_computation.6 | async-start | bytes 7356416
  182.0 23.5 %copy-start.1 = (bf16[1,3968,496]{1,2,0:T(8,128)(2,1)S(1)}, bf16[1,3968,496]{1,2,0:T(8,128)(2,1)}, u32[]{:S(2)}) copy-start(bf16[1,3968,496]{1,2,0:T(8,128)(2,1)} %param.3) | copy-start | bytes 11808772
  201.6 3.8 %collective-permute-start.2 = (bf16[8,32,1024]{2,1,0:T(8,128)(2,1)S(1)}, bf16[8,32,1024]{2,1,0:T(8,128)(2,1)S(1)}, u32[]{:S(2)}, u32[]{:S(2)}) collective-permute-start(bf16[8,32,1024]{2,1,0:T(8,128)(2,1)S(1)} %all_to_all.28.x_near_ref), channel_id=1, source_target_pairs={{0,8},{8,0},{1,9},{9,1},{2,10},{10,2},{3,11},{11,3},{4,12},{12,4},... | collective-permute-start | bytes 1572872 | tf_op jit(solution)/shard_map/rebuild/ppermute | solution.py:351
where the time goes:
time: 218 us; the launch traced here: 217 us
  blocking collectives  116 us (53%)
  Pallas kernels  70.5 us (32%)
  starting transfers between devices  12.8 us (6%)
  local copies, waits for them, and re-layouts  6.25 us (3%)
  waiting for transfers between devices  5.23 us (2%)
  matrix products  3.1 us (1%)
  other arithmetic  2.67 us (1%)
    all_to_all x2, blocking collectives, spread(): return lax.all_to_all(blocks, axes, 0, 0, tiled=True)  70.3 us
    pallas_call x1, Pallas kernels, factor(): pl.pallas_call(factor_kernel, out_shape=[jax.ShapeDtypeStruct((rank, rank...  48 us
    all_to_all x1, blocking collectives, shards(): arrived = lax.all_to_all(pair, CHIPS, 0, 0, tiled=True)  32.9 us
    all_to_all x1, blocking collectives, shards(): lax.all_to_all(part.reshape(n_sh, rank // n_sh, own), SHARD, 0, 0, tiled=...  12.5 us
    pallas_call x1, Pallas kernels, finish(): pl.pallas_call(finish_kernel, grid_spec=pltpu.PrefetchScalarGridSpec(num_...  11.5 us
    pallas_call x1, Pallas kernels, cut(): pl.pallas_call(functools.partial(cut_kernel, rows), grid_spec=pltpu.Prefe...  7.29 us
    all_to_all x1, starting transfers between devices, shards(): lax.all_to_all(w_part.reshape(n_dp, wide // n_dp, rank), DP, 0, 0, tiled=...  4.52 us
    ppermute x1, starting transfers between devices, shards(): p_far = lax.ppermute(p_near, CORE, SWAP)  4.48 us
  transfers between devices with their start and end apart: 4, of which 2 were waited for; matrix products, arithmetic and copies ran while one was open for 1% of the time, Pallas kernels for 22%

commit v1 on v0

--- a/solution.py
+++ b/solution.py
@@ -191,7 +191,16 @@
     return out
 
 
-def factor_kernel(near_hbm, far_hbm, u_ref, inverse_ref, a, near, far, held, sems):
+def packing(rank, pair):
+    at, out = 0, []
+    for i in range(rank // pair - 1):
+        size = rank - (i + 1) * pair
+        out.append((i, at, size))
+        at += size
+    return out
+
+
+def factor_kernel(near_hbm, far_hbm, packed_ref, inverse_ref, a, u_ref, near, far, held, sems):
     n_sh, n_chips, depth, width = near_hbm.shape
     rank = n_sh * depth
     near_copy = pltpu.make_async_copy(near_hbm, near, sems.at[0])
@@ -254,18 +263,22 @@
                 def _(c):
                     at = pl.multiple_of(c * pair, pair)
                     a[pl.ds(r1, pair), pl.ds(at, pair)] -= dot(ut, u_ref[pl.ds(p0, pair), pl.ds(at, pair)], rc)
+    for i, at, size in packing(rank, pair):
+        packed_ref[:, at : at + size] = u_ref[i * pair : (i + 1) * pair, rank - size :]
+
 
 def factor(near, far):
     rank = near.shape[0] * near.shape[2]
     return pl.pallas_call(
         factor_kernel,
         out_shape=[
-            jax.ShapeDtypeStruct((rank, rank), f32),
+            jax.ShapeDtypeStruct((2 * LANES, sum(size for _, _, size in packing(rank, 2 * LANES))), f32),
             jax.ShapeDtypeStruct((rank, 2 * LANES), f32),
         ],
         in_specs=[pl.BlockSpec(memory_space=pl.ANY)] * 2,
         out_specs=[pl.BlockSpec(memory_space=pltpu.VMEM)] * 2,
         scratch_shapes=[
+            pltpu.VMEM((rank, rank), f32),
             pltpu.VMEM((rank, rank), f32),
             pltpu.VMEM(near.shape, bf16),
             pltpu.VMEM(far.shape, bf16),
@@ -280,18 +293,22 @@
 
 def solve_kernel(scale, w_ref, u_ref, inverse_ref, x_ref, y, w):
     pair = 2 * LANES
-    rank = u_ref.shape[0]
+    rank = w_ref.shape[1]
     n = rank // pair
+    start = {i: at for i, at, _ in packing(rank, pair)}
     block = lambda j: slice(j * pair, (j + 1) * pair)
     for j in range(n):
         value = w_ref[:, block(j)]
-        if j:
-            value = value - dot(y[:, : j * pair], u_ref[: j * pair, block(j)], ((1,), (0,)), HIGH)
+        for i in range(j):
+            at = start[i] + (j - i - 1) * pair
+            value = value - dot(y[:, block(i)], u_ref[:, at : at + pair], ((1,), (0,)), HIGH)
         y[:, block(j)] = dot(value, inverse_ref[block(j), :], ((1,), (1,)), HIGH)
     for j in reversed(range(n)):
         value = y[:, block(j)]
         if j < n - 1:
-            value = value - dot(w[:, (j + 1) * pair :], u_ref[block(j), (j + 1) * pair :], ((1,), (1,)), HIGH)
+            value = value - dot(
+                w[:, (j + 1) * pair :], u_ref[:, start[j] : start[j] + rank - (j + 1) * pair], ((1,), (1,)), HIGH
+            )
         x = dot(value, inverse_ref[block(j), :], ((1,), (0,)), HIGH)
         w[:, block(j)] = x
         x_ref[:, block(j)] = (x * scale).astype(bf16)

time: 218 us -> 216 us (level)
  no operation moved by 1% of the time
where the time goes in v1:
time: 216 us; the launch traced here: 215 us
  blocking collectives  116 us (54%)
  Pallas kernels  70.6 us (33%)
  starting transfers between devices  12.7 us (6%)
  waiting for transfers between devices  5.23 us (2%)
  local copies, waits for them, and re-layouts  4.24 us (2%)
  matrix products  3.1 us (1%)
  other arithmetic  2.67 us (1%)
    all_to_all x2, blocking collectives, spread(): return lax.all_to_all(blocks, axes, 0, 0, tiled=True)  70.4 us
    pallas_call x1, Pallas kernels, factor(): pl.pallas_call(factor_kernel, out_shape=[jax.ShapeDtypeStruct((2 * LANES,...  48.1 us
    all_to_all x1, blocking collectives, shards(): arrived = lax.all_to_all(pair, CHIPS, 0, 0, tiled=True)  32.9 us
    all_to_all x1, blocking collectives, shards(): lax.all_to_all(part.reshape(n_sh, rank // n_sh, own), SHARD, 0, 0, tiled=...  12.5 us
    pallas_call x1, Pallas kernels, finish(): pl.pallas_call(finish_kernel, grid_spec=pltpu.PrefetchScalarGridSpec(num_...  11.5 us
    pallas_call x1, Pallas kernels, cut(): pl.pallas_call(functools.partial(cut_kernel, rows), grid_spec=pltpu.Prefe...  7.29 us
    all_to_all x1, starting transfers between devices, shards(): lax.all_to_all(w_part.reshape(n_dp, wide // n_dp, rank), DP, 0, 0, tiled=...  4.52 us
    ppermute x1, starting transfers between devices, shards(): p_far = lax.ppermute(p_near, CORE, SWAP)  4.48 us
  transfers between devices with their start and end apart: 4, of which 2 were waited for; matrix products, arithmetic and copies ran while one was open for 1% of the time, Pallas kernels for 22%

profile of v1, /device:TPU:1, one launch (start us, length us, event | category | flops | bytes accessed | tf_op | source)
XLA Modules:
  0.0 215.0 jit_solution(3930407706106079058)
XLA Ops:
  0.6 0.0 copy-start
  0.7 7.3 %cut.1 = (bf16[8,496,256]{2,1,0:T(8,128)(2,1)S(1)}, bf16[8,496,256]{2,1,0:T(8,128)(2,1)S(1)}) custom-call(s32[1]{0:T(128)} %bitcast.core_ref, bf16[496,3968]{1,0:T(8,128)(2,1)} %bitcast.30, f32[496,3968]{1,0:T(8,128)} %bitcast.26), custom_call_target="tpu_custom_call" | custom-call | tf_op jit(solution)/shard_map/total/cut/pallas_call | solution.py:56
  7.9 1.5 collective-permute-start
  9.4 3.7 %collective-permute-done = bf16[8,496,256]{2,1,0:T(8,128)(2,1)S(1)} collective-permute-done((bf16[8,496,256]{2,1,0:T(8,128)(2,1)S(1)}, bf16[8,496,256]{2,1,0:T(8,128)(2,1)S(1)}, u32[]{:S(2)}, u32[]{:S(2)}) %collective-permute-start) | collective-permute-done | bytes 2031648 | tf_op jit(solution)/shard_map/total/ppermute | solution.py:343
  13.1 0.6 add_convert_fusion
  13.7 32.9 %all_to_all.25 = bf16[8,496,256]{2,1,0:T(8,128)(2,1)S(1)} all-to-all(bf16[8,496,256]{2,1,0:T(8,128)(2,1)S(1)} %add_convert_fusion), channel_id=1, replica_groups=mesh['x'=4,'yh'=2,'c'=2,'yl'=2,'z'=4] {'x','yh'}, dimensions={0} | all-to-all | bytes 4063232 | tf_op jit(solution)/shard_map/total/all_to_all | solution.py:345
  46.7 0.3 convert_reduce_fusion
  46.9 0.0 copy-done
  46.9 1.0 fusion
  48.0 0.1 copy.11
  48.1 12.5 %all_to_all.26 = bf16[8,128,256]{1,2,0:T(8,128)(2,1)S(1)} all-to-all(bf16[8,128,256]{1,2,0:T(8,128)(2,1)S(1)} %bitcast.33), channel_id=1, replica_groups=mesh['x'=4,'yh'=2,'c'=2,'yl'=2,'z'=4] {'yl','z'}, dimensions={0} | all-to-all | bytes 1048576 | tf_op jit(solution)/shard_map/left/all_to_all | solution.py:350
  60.5 0.1 reduce_sum.31
  60.6 0.1 copy.7
  60.7 0.5 broadcast_in_dim.9
  61.2 54.4 %all_to_all.27 = bf16[64,128,256]{2,1,0:T(8,128)(2,1)} all-to-all(bf16[64,128,256]{2,1,0:T(8,128)(2,1)S(1)} %broadcast_in_dim.9), channel_id=1, replica_groups=mesh['x'=4,'yh'=2,'c'=2,'yl'=2,'z'=4] {'yl','z','x','yh'}, dimensions={0} | all-to-all | bytes 8388608 | tf_op jit(solution)/shard_map/left/all_to_all | solution.py:31
  115.6 4.5 %collective-permute-start.1 = (bf16[8,8,128,256]{3,2,1,0:T(8,128)(2,1)}, bf16[8,8,128,256]{3,2,1,0:T(8,128)(2,1)}, u32[]{:S(2)}, u32[]{:S(2)}) collective-permute-start(bf16[8,8,128,256]{3,2,1,0:T(8,128)(2,1)} %bitcast.6.near_hbm.near_ref), channel_id=1, source_target_pairs={{0,8},{8,0},{1,9},{9,1},{2,10},{10,2},{3,11},{11,3},{4,12},{12,4},... | collective-permute-start | bytes 12582920 | tf_op jit(solution)/shard_map/left/ppermute | solution.py:353
  120.1 1.1 constant_dynamic-slice_fusion
  121.2 2.1 fusion.1
  123.3 4.5 %all-to-all-start.3 = ((f32[16,32,1024]{2,1,0:T(8,128)}), f32[16,32,1024]{2,1,0:T(8,128)}, u32[]{:S(2)}, u32[]{:S(2)}) async-start(f32[16,32,1024]{2,1,0:T(8,128)} %fusion.1), calls=%async_computation.3 | async-start | bytes 4194304 | tf_op jit(solution)/shard_map/right/all_to_all | solution.py:359
  127.8 0.0 collective-permute-done.1.far_hbm.far_ref
  127.8 48.1 %factor.1 = (f32[256,1536]{1,0:T(8,128)S(1)}, f32[1024,256]{1,0:T(8,128)S(1)}) custom-call(bf16[8,8,128,256]{3,2,1,0:T(8,128)(2,1)} %bitcast.6.near_hbm.near_ref, bf16[8,8,128,256]{3,2,1,0:T(8,128)(2,1)} %collective-permute-done.1.far_hbm.far_ref), custom_call_target="tpu_custom_call" | custom-call | flops 60000002048 | bytes 8388608 | tf_op jit(solution)/shard_map/solve/factor/pallas_call | solution.py:272
  175.9 0.0 copy-start.2
  176.0 1.0 copy-done.2
  176.9 0.0 all-to-all-done.3
  176.9 1.7 reduce_sum.32.w_ref
  178.6 0.0 slice-start
  178.7 0.0 copy-start.3
  178.7 1.4 copy-done.3
  180.0 0.0 slice-start.1
  180.0 0.0 copy-start.1
  180.0 3.6 %solve.1 = bf16[32,1024]{1,0:T(8,128)(2,1)S(1)} custom-call(f32[32,1024]{1,0:T(8,128)S(1)} %reduce_sum.32.w_ref, f32[256,1536]{1,0:T(8,128)S(1)} %get-tuple-element.14.u_ref, f32[1024,256]{1,0:T(8,128)S(1)} %copy-done.3), custom_call_target="tpu_custom_call" | custom-call | flops 8000000000 | bytes 16777216 | tf_op jit(solution)/shard_map/solve/solve/pallas_call | solution.py:318
  183.7 0.1 broadcast_in_dim.10
  183.7 16.0 %all_to_all.28.x_near_ref = bf16[8,32,1024]{2,1,0:T(8,128)(2,1)S(1)} all-to-all(bf16[8,32,1024]{2,1,0:T(8,128)(2,1)S(1)} %broadcast_in_dim.10), channel_id=1, replica_groups=mesh['x'=4,'yh'=2,'c'=2,'yl'=2,'z'=4] {'x','yh'}, dimensions={0} | all-to-all | bytes 1048576 | tf_op jit(solution)/shard_map/rebuild/all_to_all | solution.py:31
  199.7 2.2 %collective-permute-start.2 = (bf16[8,32,1024]{2,1,0:T(8,128)(2,1)S(1)}, bf16[8,32,1024]{2,1,0:T(8,128)(2,1)S(1)}, u32[]{:S(2)}, u32[]{:S(2)}) collective-permute-start(bf16[8,32,1024]{2,1,0:T(8,128)(2,1)S(1)} %all_to_all.28.x_near_ref), channel_id=1, source_target_pairs={{0,8},{8,0},{1,9},{9,1},{2,10},{10,2},{3,11},{11,3},{4,12},{12,4},... | collective-permute-start | bytes 1572872 | tf_op jit(solution)/shard_map/rebuild/ppermute | solution.py:368
  202.0 1.5 collective-permute-done.2.x_far_ref
  203.5 0.0 slice-done
  203.5 0.0 slice-done.1
  203.5 0.0 copy-done.1
  203.5 11.5 %finish.1 = (bf16[496,3968]{1,0:T(8,128)(2,1)}, f32[496,3968]{1,0:T(8,128)}) custom-call(s32[1]{0:T(128)} %bitcast.core_ref, bf16[8,8,128,256]{3,2,1,0:T(8,128)(2,1)} %bitcast.6.near_hbm.near_ref, bf16[8,8,128,256]{3,2,1,0:T(8,128)(2,1)} %collective-permute-done.1.far_hbm.far_ref, bf16[8,32,1024]{2,1,0:T(8,128)(2,1)S(1)} %all_to_all.28.x_near_ref, ...), custom_call_target="tpu_custom_call" | custom-call | tf_op jit(solution)/shard_map/rebuild/finish/pallas_call | solution.py:103
  (2 shorter events, 0.0 us)
Async XLA Ops:
  0.6 46.3 %copy-start = (bf16[496,1024]{1,0:T(8,128)(2,1)S(1)}, bf16[496,1024]{1,0:T(8,128)(2,1)}, u32[]{:S(2)}) copy-start(bf16[496,1024]{1,0:T(8,128)(2,1)} %param.5) | copy-start | bytes 3047428
  7.9 5.2 %collective-permute-start = (bf16[8,496,256]{2,1,0:T(8,128)(2,1)S(1)}, bf16[8,496,256]{2,1,0:T(8,128)(2,1)S(1)}, u32[]{:S(2)}, u32[]{:S(2)}) collective-permute-start(bf16[8,496,256]{2,1,0:T(8,128)(2,1)S(1)} %get-tuple-element.11), channel_id=1, source_target_pairs={{0,8},{8,0},{1,9},{9,1},{2,10},{10,2},{3,11},{11,3},{4,12},{12,4},... | collective-permute-start | bytes 6094856 | tf_op jit(solution)/shard_map/total/ppermute | solution.py:343
  115.6 12.2 %collective-permute-start.1 = (bf16[8,8,128,256]{3,2,1,0:T(8,128)(2,1)}, bf16[8,8,128,256]{3,2,1,0:T(8,128)(2,1)}, u32[]{:S(2)}, u32[]{:S(2)}) collective-permute-start(bf16[8,8,128,256]{3,2,1,0:T(8,128)(2,1)} %bitcast.6.near_hbm.near_ref), channel_id=1, source_target_pairs={{0,8},{8,0},{1,9},{9,1},{2,10},{10,2},{3,11},{11,3},{4,12},{12,4},... | collective-permute-start | bytes 12582920 | tf_op jit(solution)/shard_map/left/ppermute | solution.py:353
  123.3 53.6 %all-to-all-start.3 = ((f32[16,32,1024]{2,1,0:T(8,128)}), f32[16,32,1024]{2,1,0:T(8,128)}, u32[]{:S(2)}, u32[]{:S(2)}) async-start(f32[16,32,1024]{2,1,0:T(8,128)} %fusion.1), calls=%async_computation.3 | async-start | bytes 4194304 | tf_op jit(solution)/shard_map/right/all_to_all | solution.py:359
  175.9 1.0 copy-start.2
  178.6 24.9 %slice-start = ((s8[7872512]{0:T(1024)(128)(4,1)}), s8[4194304]{0:T(1024)(128)(4,1)S(1)}, s32[]{:S(2)}) async-start(s8[7872512]{0:T(1024)(128)(4,1)} %bitcast.27), calls=%async_computation.5 | async-start | bytes 8388608
  178.7 1.4 copy-start.3
  180.0 23.5 %slice-start.1 = ((s8[7872512]{0:T(1024)(128)(4,1)}), s8[3678208]{0:T(1024)(128)(4,1)S(1)}, s32[]{:S(2)}) async-start(s8[7872512]{0:T(1024)(128)(4,1)} %bitcast.27), calls=%async_computation.6 | async-start | bytes 7356416
  180.0 23.5 %copy-start.1 = (bf16[1,3968,496]{1,2,0:T(8,128)(2,1)S(1)}, bf16[1,3968,496]{1,2,0:T(8,128)(2,1)}, u32[]{:S(2)}) copy-start(bf16[1,3968,496]{1,2,0:T(8,128)(2,1)} %param.3) | copy-start | bytes 11808772
  199.7 3.8 %collective-permute-start.2 = (bf16[8,32,1024]{2,1,0:T(8,128)(2,1)S(1)}, bf16[8,32,1024]{2,1,0:T(8,128)(2,1)S(1)}, u32[]{:S(2)}, u32[]{:S(2)}) collective-permute-start(bf16[8,32,1024]{2,1,0:T(8,128)(2,1)S(1)} %all_to_all.28.x_near_ref), channel_id=1, source_target_pairs={{0,8},{8,0},{1,9},{9,1},{2,10},{10,2},{3,11},{11,3},{4,12},{12,4},... | collective-permute-start | bytes 1572872 | tf_op jit(solution)/shard_map/rebuild/ppermute | solution.py:368
